TPU v7x, 768 devices: a whole 4x8x12 slice. The times are simulated.
768 devices in a mesh: row: 48 (over z, y_lo), col: 4 (over y_hi, core), dep: 4 (over x).
Axes of the slice: x: 4, y: 8 (y_hi: 2, y_lo: 4; y = y_hi * 4 + y_lo), z: 12, core: 2. Of those that a mesh axis runs over, the one named last changes fastest.
Arguments:
- amp_old: bfloat16 [960, 2, 480], P('row', None, 'dep'), may hold values from -6 to 6
- ladder_int: bfloat16 [480, 480, 2, 480], P('row', 'col', None, 'dep'), may hold values from -0.5 to 0.5
- cycle_int: bfloat16 [60, 64, 480], replicated, may hold values from -0.03125 to 0.03125
- virt_irrep: int32 [480], replicated, may hold values from 0 to 7
- occ_energy: float32 [60], replicated, may hold values from -3 to -0.5
- virt_energy: float32 [480], replicated, may hold values from 0.5 to 3
Outputs:
- new_amps: bfloat16 [16, 60, 480, 480], P(('col', 'dep'), None, 'row')
- cycle_term: float32 [16, 480, 64], P(('col', 'dep'), 'row')
All inputs are finite; a program needn't handle non-finite values.
Results may differ from a plain program's by a relative error of at most 0.015.
Values may be sent and summed in bfloat16 or wider, within the bound.
A program may use at most 32 MiB of HBM per device.

v0:
```python
import jax
import jax.numpy as jnp
from jax import lax
from jax.sharding import PartitionSpec as P


def on_device(amp_old, ladder_int, cycle_int, virt_irrep, occ_energy, virt_energy):
    a_loc, b_loc, panel, d_loc = ladder_int.shape
    n_col = lax.axis_size("col")
    n_dep = lax.axis_size("dep")
    row_idx = lax.axis_index("row")
    col_idx = lax.axis_index("col")
    dep_idx = lax.axis_index("dep")
    lab_a = lax.dynamic_slice_in_dim(virt_irrep, row_idx * a_loc, a_loc)
    lab_b = lax.dynamic_slice_in_dim(virt_irrep, col_idx * b_loc, b_loc)
    lab_d = lax.dynamic_slice_in_dim(virt_irrep, dep_idx * d_loc, d_loc)
    lab_c = virt_irrep[:panel]
    sym = (
        jnp.bitwise_xor(
            jnp.bitwise_xor(lab_a[:, None, None, None], lab_b[None, :, None, None]),
            jnp.bitwise_xor(lab_c[None, None, :, None], lab_d[None, None, None, :]),
        )
        == 0
    )
    masked = jnp.where(sym, ladder_int, jnp.zeros((), jnp.bfloat16))
    w_matrix = masked.reshape(a_loc * b_loc, panel * d_loc)
    piece = lax.all_gather(amp_old, "row", axis=0, tiled=True)
    left = piece.reshape(piece.shape[0], panel * d_loc)
    partial_sums = lax.dot_general(
        left, w_matrix, (((1,), (1,)), ((), ())), preferred_element_type=jnp.float32
    )
    n_occ = occ_energy.shape[0]
    i_loc = partial_sums.shape[0] // (n_occ * n_col * n_dep)
    partial_sums = partial_sums.reshape(n_col, n_dep, i_loc, n_occ, a_loc, b_loc)
    summed = lax.psum_scatter(
        partial_sums.astype(jnp.bfloat16), "dep", scatter_dimension=1, tiled=True
    ).astype(jnp.float32)
    col_ids = jnp.arange(n_col, dtype=jnp.int32)[:, None]
    loc_ids = jnp.arange(i_loc, dtype=jnp.int32)[None, :]
    occ_ids = col_ids * (n_dep * i_loc) + dep_idx * i_loc + loc_ids
    occ_i = occ_energy[occ_ids]
    ene_a = lax.dynamic_slice_in_dim(virt_energy, row_idx * a_loc, a_loc)
    ene_b = lax.dynamic_slice_in_dim(virt_energy, col_idx * b_loc, b_loc)
    denom = (
        ene_a[None, None, None, None, :, None]
        + ene_b[None, None, None, None, None, :]
        - occ_i[:, None, :, None, None, None]
        - occ_energy[None, None, None, :, None, None]
    )
    amps = (summed / denom).astype(jnp.bfloat16)
    moved = lax.all_to_all(amps, "col", split_axis=0, concat_axis=5, tiled=True)
    new_amps = moved.reshape(i_loc, n_occ, a_loc, n_col * b_loc)
    cycle_term = jnp.einsum(
        "ikac,kqc->iaq", new_amps, cycle_int, preferred_element_type=jnp.float32
    )
    return (new_amps, cycle_term)


def solution(mesh):
    placed = (P("row", None, "dep"), P("row", "col", None, "dep"), P(), P(), P(), P())
    return jax.shard_map(
        on_device,
        mesh=mesh,
        in_specs=placed,
        out_specs=(P(("col", "dep"), None, "row", None), P(("col", "dep"), "row", None)),
        check_vma=False,
    )
```

profile of v0, /device:TPU:1, one launch (start us, length us, event | category | flops | bytes accessed | tf_op | source)
XLA Modules:
  0.0 277.7 jit_solution(12698442693046437149)
XLA Ops:
  7.2 0.0 copy-start.1
  7.2 0.0 all-reduce.3.cloned.1.call-start
  7.2 0.7 slice.3
  7.9 0.8 dynamic_slice.15
  8.7 0.8 fusion.3
  9.5 0.1 broadcast_xor_fusion
  9.6 0.1 broadcast_xor_fusion.1
  9.6 5.0 %compare_select_fusion = bf16[10,120,2,120]{3,2,1,0:T(2,128)(2,1)S(1)} fusion(bf16[10,120,2,120]{3,2,1,0:T(2,128)(2,1)} %param.7, s32[2,120]{1,0:T(2,128)S(1)} %broadcast_xor_fusion.1, s32[10,120]{1,0:T(8,128)S(1)} %broadcast_xor_fusion), kind=kLoop, calls=%fused_computation.3 | loop fusion | flops 864000 | bytes 1157760 | tf_op jit(solution)/shard_map/jit(_where)/select_n | solution.py:25
  14.7 0.4 reshape.170
  15.1 107.3 %all_gather.3 = bf16[960,2,120]{2,1,0:T(2,128)(2,1)S(1)} all-gather(bf16[20,2,120]{2,1,0:T(2,128)(2,1)S(1)} %copy-done.1), channel_id=1, replica_groups=mesh['row'=48,'col'=4,'dep'=4] {'row'}, dimensions={0}, use_global_device_ids=true | all-gather | bytes 470400 | tf_op jit(solution)/shard_map/all_gather | solution.py:27
  122.4 1.1 reshape.171
  123.5 1.9 fusion
  125.4 9.0 %reshape.184 = bf16[4,4,1,60,10,120]{3,1,0,5,4,2:T(4,128)(2,1)} reshape(bf16[960,1200]{0,1:T(8,128)(2,1)S(1)} %fusion) | data formatting | bytes 4608000 | tf_op jit(solution)/shard_map/convert_element_type | solution.py:36
  134.4 9.3 %copy.24 = bf16[4,4,1,60,10,120]{5,0,4,3,2,1:T(4,128)(2,1)} copy(bf16[4,4,1,60,10,120]{3,1,0,5,4,2:T(4,128)(2,1)} %reshape.184) | data formatting | bytes 4608000 | tf_op jit(solution)/shard_map/convert_element_type | solution.py:36
  143.8 0.0 all-reduce.3.cloned.1.call-update
  143.8 0.7 copy-done.2
  144.5 0.1 dynamic_slice.18
  144.5 0.1 dynamic_slice.19
  144.6 0.6 gather_fusion
  145.3 1.3 dynamic-slice
  146.5 0.1 broadcast_add_fusion
  146.6 0.1 broadcast_subtract_fusion
  146.7 90.8 %all-reduce.3.cloned.1.call-done = bf16[4,4,1,60,10,120]{5,0,4,3,2,1:T(4,128)(2,1)} async-done(((bf16[4,4,1,60,10,120]{5,0,4,3,2,1:T(4,128)(2,1)}), bf16[4,4,1,60,10,120]{5,0,4,3,2,1:T(4,128)(2,1)}) %all-reduce.3.cloned.1.call-update) | async-done | bytes 2304016
  237.5 2.2 fusion.1
  239.7 0.2 copy.25
  239.8 24.4 %all_to_all.15 = bf16[4,1,1,60,10,120]{5,3,4,2,1,0:T(8,128)(2,1)S(1)} all-to-all(bf16[4,1,1,60,10,120]{5,3,4,2,1,0:T(8,128)(2,1)S(1)} %copy.25), channel_id=1, replica_groups=mesh['row'=48,'col'=4,'dep'=4] {'col'}, dimensions={0} | all-to-all | bytes 1152000 | tf_op jit(solution)/shard_map/all_to_all | solution.py:51
  264.2 0.5 copy.35
  264.7 0.2 copy.27
  264.9 0.6 reshape.185
  265.6 1.4 reshape.172
  267.0 3.2 %convolution_bitcast_fusion = f32[1,10,64]{2,1,0:T(8,128)S(1)} fusion(bf16[60,10,480]{2,1,0:T(8,128)(2,1)S(1)} %reshape.185, bf16[60,64,480]{2,1,0:T(8,128)(2,1)} %param.8), kind=kOutput, calls=%fused_computation.6 | convolution fusion | flops 36864000 | bytes 4264960 | tf_op jit(solution)/shard_map/ikac,kqc->iaq/dot_general | solution.py:53
  270.2 0.6 copy.30
  (6 shorter events, 0.0 us)
Async XLA Ops:
  7.2 7.9 %copy-start.1 = (bf16[20,2,120]{2,1,0:T(2,128)(2,1)S(1)}, bf16[20,2,120]{2,1,0:T(2,128)(2,1)}, u32[]{:S(2)}) copy-start(bf16[20,2,120]{2,1,0:T(2,128)(2,1)} %param.6) | copy-start | bytes 28804
  7.2 230.3 %all-reduce.3.cloned.1.call-start = ((), (), s32[]{:S(2)}) async-start(), calls=%async_computation.1 | async-start | bytes 4915200
  143.8 0.7 copy-start.2
  143.8 0.8 copy-start
Sparse Core Ops, SparseCore 0:
  143.9 93.4 all-reduce.2
where the time goes:
time: 280 us; the launch traced here: 278 us
  blocking collectives  132 us (47%)
  waiting for transfers between devices  90.8 us (32%)
  local copies, waits for them, and re-layouts  28.3 us (10%)
  between operations  14.1 us (5%)
  other arithmetic  7.54 us (3%)
  matrix products  5.09 us (2%)
    all_gather x1, blocking collectives, on_device(): piece = lax.all_gather(amp_old, 'row', axis=0, tiled=True)  107 us
    unnamed x2, waiting for transfers between devices  90.8 us
    all_to_all x1, blocking collectives, on_device(): moved = lax.all_to_all(amps, 'col', split_axis=0, concat_axis=5, tiled=True)  24.4 us
    convert_element_type x2, local copies, waits for them, and re-layouts, on_device(): partial_sums.astype(jnp.bfloat16)  18.4 us
  transfers between devices with their start and end apart: 1, of which 1 were waited for; matrix products, arithmetic and copies ran while one was open for 1% of the time, Pallas kernels for 0%

commit v1 on v0

v1 whole, which is shorter than its diff:
```python
import jax
import jax.numpy as jnp
from jax import lax
from jax.experimental import pallas as pl
from jax.experimental.pallas import tpu as pltpu
from jax.sharding import PartitionSpec as P

MESH = pl.DeviceIdType.MESH
F32 = jnp.float32
BF16 = jnp.bfloat16
NX, NY, NZ = 4, 4, 12
NA, NB_, ND, NK, NQ = 10, 120, 120, 60, 64
CH = 5
KD = 2 * ND


def kernel(
    amp_ref, lad_ref, cyc_hbm, irr_s, ene_s, irr_ref, occ_ref, ene_ref,
    out_ref, z_ref,
    vec_f, vec_i, shard, sh_all, lt, a_f, a_b, nb, rb, of, cyc, crot, zp, zr,
    cyc_sem, own_sem, s1_send, s1_recv, s2_send, s2_recv, x_send, x_recv, e_send, e_recv, z_send, z_recv,
):
    row = lax.axis_index("row")
    col = lax.axis_index("col")
    x = lax.axis_index("dep")
    z = row // 4
    y = row % 4
    yh = col // 2
    core = col % 2

    def dev(zz, yy, cc, xx):
        return (zz * 4 + yy, cc, xx)

    r12 = 4 * (z % 3) + y
    xt = r12 // 3
    s_mine = r12 % 3
    ip_mine = z // 3
    s_here = (x + y) % 4
    z_off = (3 * x + s_here) // 4
    relay = s_here < 3

    left = (x + 3) % 4
    right = (x + 1) % 4
    diag = (x + 2) % 4

    barrier = pltpu.get_barrier_semaphore()

    def signal(d):
        pl.semaphore_signal(barrier, inc=1, device_id=d, device_id_type=MESH)

    @pl.when(relay)
    def _():
        def go(n, carry):
            i4 = n // 4
            xx = n % 4
            zz = 3 * i4 + z_off

            @pl.when(jnp.logical_or(zz != z, xx != x))
            def _():
                signal(dev(zz, y, col, xx))

            return carry

        lax.fori_loop(0, 16, go, 0)

    for t in range(1, 4):
        signal(dev(z, (y + t) % 4, col, x))
    signal(dev(z, y, col, left))
    signal(dev(z, y, col, right))
    for t in range(1, 4):
        signal(dev(z, y, (col + t) % 4, x))

    cyc_copy = pltpu.make_async_copy(cyc_hbm, cyc, cyc_sem)
    cyc_copy.start()

    raw = amp_ref[...]
    wide = jnp.concatenate(
        [raw[:, 0, :].astype(F32), raw[:, 1, :].astype(F32), jnp.zeros((20, 16), F32)], axis=1
    )
    gap = jnp.zeros((4, 128), F32)
    shard[...] = jnp.concatenate([wide[:, :128], gap, wide[:, 128:], gap], axis=0).astype(BF16)

    vec_f[...] = jnp.zeros_like(vec_f)
    vec_i[...] = jnp.zeros_like(vec_i)
    vec_f[0:1, 0:480] = ene_ref[...]
    vec_f[1:2, 0:60] = occ_ref[...]
    vec_i[0:1, 0:480] = irr_ref[...]
    lane = lax.broadcasted_iota(jnp.int32, (1, 128), 1)
    edge = 120 - 8 * col
    prev = jnp.maximum(col - 1, 0)
    at = pl.multiple_of(col * 128, 128)
    before = pl.multiple_of(prev * 128, 128)
    ene_b = jnp.where(lane < edge, vec_f[0:1, pl.ds(at, 128)], vec_f[0:1, pl.ds(before, 128)])
    irr_b = jnp.where(lane < edge, vec_i[0:1, pl.ds(at, 128)], vec_i[0:1, pl.ds(before, 128)])
    ii = lax.broadcasted_iota(jnp.int32, (ND, 512), 0)
    jj = lax.broadcasted_iota(jnp.int32, (ND, 512), 1)
    irr_d = jnp.sum(jnp.where(jj == ii + ND * x, vec_i[0:1, :].astype(F32), 0.0), axis=1, keepdims=True).astype(jnp.int32)
    pi = lax.broadcasted_iota(jnp.int32, (256, 128), 0)
    pj = lax.broadcasted_iota(jnp.int32, (256, 128), 1)
    occ_row = vec_f[1:2, 0:128]
    occ_i = jnp.sum(jnp.where(pj == (pi // 64) * 4 + x, occ_row, 0.0), axis=1, keepdims=True)
    occ_k = jnp.sum(jnp.where(pj == pi % 64, occ_row, 0.0), axis=1, keepdims=True)
    pair_occ = occ_i + occ_k

    sr = lax.broadcasted_iota(jnp.int32, (2 * NB_, 256), 0)
    sc = lax.broadcasted_iota(jnp.int32, (2 * NB_, 256), 1)
    want_b = (sc % 128 + 8 * col) % 128
    pick = jnp.where(sr == 2 * want_b + sc // 128, 1.0, 0.0).astype(BF16)

    def prep(a, carry):
        block = lad_ref[pl.ds(pl.multiple_of(a * 240, 240), 240), :]
        got = lax.dot_general(block, pick, (((0,), (0,)), ((), ())), preferred_element_type=F32)
        ab = jnp.bitwise_xor(irr_b, irr_s[row * NA + a])
        both = []
        for c in range(2):
            keep = jnp.bitwise_xor(ab, irr_s[c]) == irr_d
            both.append(jnp.where(keep, got[:, c * 128:(c + 1) * 128], 0.0))
        lt[x, a] = jnp.concatenate(both, axis=0).astype(BF16)
        return carry

    lax.fori_loop(0, NA, prep, 0)
    a_f[...] = jnp.zeros_like(a_f)

    pl.semaphore_wait(barrier, 8 + 12 - jnp.where(xt == x, 1, 0))

    def s1_copy(zz):
        return pltpu.make_async_remote_copy(
            src_ref=shard, dst_ref=sh_all.at[s_mine, ip_mine, x],
            send_sem=s1_send.at[zz], recv_sem=s1_recv.at[ip_mine, x],
            device_id=dev(zz, y, col, xt), device_id_type=MESH,
        )

    def s1_here(zz):
        return jnp.logical_and(zz == z, xt == x)

    def s1_go(n, carry):
        zz = (z + jnp.where(n % 2 == 0, 6 - n // 2, 12 - 5 + n // 2)) % 12

        @pl.when(jnp.logical_not(s1_here(zz)))
        def _():
            s1_copy(zz).start()

        return carry

    lax.fori_loop(0, 12, s1_go, 0)

    @pl.when(xt == x)
    def _():
        pltpu.make_async_copy(shard, sh_all.at[s_mine, ip_mine, x], own_sem).start()

    def x_own(j, side):
        return pltpu.make_async_remote_copy(
            src_ref=lt.at[x, pl.ds(2 * j, 2)], dst_ref=lt.at[x, pl.ds(2 * j, 2)],
            send_sem=x_send.at[side, j], recv_sem=x_recv.at[side, j],
            device_id=dev(z, y, col, left if side == 0 else right), device_id_type=MESH,
        )

    def x_fwd(j, side):
        owner = right if side == 0 else left
        a = 2 * j + (1 if side == 0 else 0)
        return pltpu.make_async_remote_copy(
            src_ref=lt.at[owner, a], dst_ref=lt.at[owner, a],
            send_sem=x_send.at[2 + side, j], recv_sem=x_recv.at[2 + side, j],
            device_id=dev(z, y, col, left if side == 0 else right), device_id_type=MESH,
        )

    for j in range(3):
        x_own(j, 0).start()
        x_own(j, 1).start()

    cyc_copy.wait()
    lane3 = lax.broadcasted_iota(jnp.int32, (1, 1, 128), 2)
    for t in range(4):
        @pl.when(col == t)
        def _():
            def rot(k, carry):
                lo = max(t - 1, 0) * 128
                if t < 3:
                    here = cyc[pl.ds(k, 1), :, t * 128:(t + 1) * 128]
                else:
                    here = jnp.concatenate(
                        [cyc[pl.ds(k, 1), :, 384:480], cyc[pl.ds(k, 1), :, 352:384]], axis=2
                    )
                there = cyc[pl.ds(k, 1), :, lo:lo + 128]
                crot[pl.ds(k, 1)] = jnp.where(lane3 < 120 - 8 * t, here, there)
                return carry

            lax.fori_loop(0, NK, rot, 0)

    def s2_copy(t, h):
        half = (1 - yh) if h == 0 else yh
        return pltpu.make_async_remote_copy(
            src_ref=sh_all.at[s_here, pl.ds(2 * half, 2)], dst_ref=sh_all.at[s_here, pl.ds(2 * half, 2)],
            send_sem=s2_send.at[t - 1, h], recv_sem=s2_recv.at[s_here, h],
            device_id=dev(z, (y + t) % 4, col, x), device_id_type=MESH,
        )

    @pl.when(relay)
    def _():
        def got(n, carry):
            i4 = n // 4
            xx = n % 4
            zz = 3 * i4 + z_off

            @pl.when(jnp.logical_or(zz != z, xx != x))
            def _():
                pltpu.make_async_remote_copy(
                    src_ref=shard, dst_ref=sh_all.at[s_here, i4, xx],
                    send_sem=s1_send.at[0], recv_sem=s1_recv.at[i4, xx],
                    device_id=dev(z, y, col, x), device_id_type=MESH,
                ).wait_recv()

            return carry

        lax.fori_loop(0, 16, got, 0)

    @pl.when(xt == x)
    def _():
        pltpu.make_async_copy(shard, sh_all.at[s_mine, ip_mine, x], own_sem).wait()

    @pl.when(relay)
    def _():
        for h in range(2):
            for t in (2, 1, 3):
                s2_copy(t, h).start()

    def forward(j):
        x_own(j, 0).wait_recv()
        x_own(j, 1).wait_recv()
        x_fwd(j, 0).start()
        x_fwd(j, 1).start()
        if j + 3 < CH:
            x_own(j + 3, 0).start()
            x_own(j + 3, 1).start()

    forward(0)
    forward(1)

    def s2_wait(s, h):
        half = (1 - yh) if h == 0 else yh
        pltpu.make_async_remote_copy(
            src_ref=sh_all.at[s, pl.ds(2 * half, 2)], dst_ref=sh_all.at[s, pl.ds(2 * half, 2)],
            send_sem=s2_send.at[0, h], recv_sem=s2_recv.at[s, h],
            device_id=dev(z, y, col, x), device_id_type=MESH,
        ).wait_recv()

    for h in range(2):
        for s in range(3):
            @pl.when(s_here != s)
            def _():
                s2_wait(s, h)

    for xx in range(4):
        for i4 in range(4):
            for s in range(3):
                got = sh_all[s, i4, xx].astype(F32)
                top = i4 * 64 + s * 20
                a_f[top:top + 20, 0:128] = got[0:20]
                a_f[top:top + 20, 128:256] = got[24:44]
        a_b[xx] = a_f[...].astype(BF16)

    partners = [(2, 0), (2, 1), (0, 1)]

    def e_copy(p, j):
        dh, dc = partners[p]
        to = ((yh * 2 + dh) % 4) + (core + dc) % 2
        return pltpu.make_async_remote_copy(
            src_ref=nb.at[to, pl.ds(2 * j, 2)], dst_ref=rb.at[col, pl.ds(2 * j, 2)],
            send_sem=e_send.at[p, j], recv_sem=e_recv.at[p, j],
            device_id=dev(z, y, to, x), device_id_type=MESH,
        )

    def e_wait(p, j):
        dh, dc = partners[p]
        frm = ((yh * 2 + dh) % 4) + (core + dc) % 2
        pltpu.make_async_remote_copy(
            src_ref=nb.at[frm, pl.ds(2 * j, 2)], dst_ref=rb.at[frm, pl.ds(2 * j, 2)],
            send_sem=e_send.at[p, j], recv_sem=e_recv.at[p, j],
            device_id=dev(z, y, frm, x), device_id_type=MESH,
        ).wait_recv()

    for j in range(CH):
        if j + 2 < CH:
            forward(j + 2)
        x_fwd(j, 0).wait_recv()
        x_fwd(j, 1).wait_recv()
        total = None
        for xx in range(4):
            w = jnp.concatenate([lt[xx, 2 * j], lt[xx, 2 * j + 1]], axis=1)
            term = jnp.dot(a_b[xx, :, 0:KD], w, preferred_element_type=F32)
            total = term if total is None else total + term
        for h in range(2):
            a = 2 * j + h
            denom = (ene_s[row * NA + a] + ene_b) - pair_occ
            new = (total[:, h * 128:(h + 1) * 128] / denom).astype(BF16)
            for i4 in range(4):
                nb[i4, a] = new[i4 * 64:(i4 + 1) * 64]
            of[a * 256:(a + 1) * 256, :] = new.astype(F32)
        for p in range(3):
            e_copy(p, j).start()

    rb[pl.ds(col, 1)] = nb[pl.ds(col, 1)]

    def cycle(k, acc):
        rows = []
        for i4 in range(4):
            rows.append(of[pl.ds(i4 * 64 + k, 10, stride=256), :])
            rows.append(jnp.zeros((6, 128), F32))
        left_op = jnp.concatenate(rows, axis=0).astype(BF16)
        return acc + lax.dot_general(left_op, crot[k], (((1,), (1,)), ((), ())), preferred_element_type=F32)

    zsum = lax.fori_loop(0, NK, cycle, jnp.zeros((64, NQ), F32))
    zw = jnp.concatenate([zsum, jnp.zeros((64, 64), F32)], axis=1)
    for i4 in range(4):
        zp[i4] = zw[i4 * 16:(i4 + 1) * 16]
    zr[pl.ds(col, 1)] = zp[pl.ds(col, 1)]

    def z_copy(p):
        dh, dc = partners[p]
        to = ((yh * 2 + dh) % 4) + (core + dc) % 2
        return pltpu.make_async_remote_copy(
            src_ref=zp.at[to], dst_ref=zr.at[col],
            send_sem=z_send.at[p], recv_sem=z_recv.at[p],
            device_id=dev(z, y, to, x), device_id_type=MESH,
        )

    def z_wait(p):
        dh, dc = partners[p]
        frm = ((yh * 2 + dh) % 4) + (core + dc) % 2
        pltpu.make_async_remote_copy(
            src_ref=zp.at[frm], dst_ref=zr.at[frm],
            send_sem=z_send.at[p], recv_sem=z_recv.at[p],
            device_id=dev(z, y, frm, x), device_id_type=MESH,
        ).wait_recv()

    for p in range(3):
        z_copy(p).start()

    lane_o = lax.broadcasted_iota(jnp.int32, (1, 128), 1)
    for j in range(CH):
        for p in range(3):
            e_wait(p, j)
        for h in range(2):
            a = 2 * j + h
            for t in range(3):
                tile = jnp.where(lane_o < 120 - 8 * t, rb[t, a], rb[t + 1, a])
                out_ref[a, :, t * 128:(t + 1) * 128] = tile[:NK]
            out_ref[a, :, 384:480] = rb[3, a][:NK, :96]

    for p in range(3):
        z_wait(p)
    zt = (zr[0] + zr[1]) + (zr[2] + zr[3])
    z_ref[...] = zt[:NA, :NQ]

    def s1_done(zz, carry):
        @pl.when(jnp.logical_not(s1_here(zz)))
        def _():
            s1_copy(zz).wait_send()

        return carry

    lax.fori_loop(0, 12, s1_done, 0)

    @pl.when(relay)
    def _():
        for h in range(2):
            for t in range(1, 4):
                s2_copy(t, h).wait_send()

    for j in range(CH):
        for side in range(2):
            x_own(j, side).wait_send()
            x_fwd(j, side).wait_send()
        for p in range(3):
            e_copy(p, j).wait_send()
    for p in range(3):
        z_copy(p).wait_send()


def on_device(amp_old, ladder_int, cycle_int, virt_irrep, occ_energy, virt_energy):
    vmem = pl.BlockSpec(memory_space=pltpu.VMEM)
    smem = pl.BlockSpec(memory_space=pltpu.SMEM)
    dma = pltpu.SemaphoreType.DMA
    lad = ladder_int.reshape(2 * NA * NB_, ND)
    amps, cyc = pl.pallas_call(
        kernel,
        name="ladder",
        out_shape=(
            jax.ShapeDtypeStruct((NA, NK, 480), BF16),
            jax.ShapeDtypeStruct((NA, NQ), F32),
        ),
        in_specs=[vmem, vmem, pl.BlockSpec(memory_space=pl.ANY), smem, smem, vmem, vmem, vmem],
        out_specs=(vmem, vmem),
        scratch_shapes=[
            pltpu.VMEM((8, 512), F32),
            pltpu.VMEM((8, 512), jnp.int32),
            pltpu.VMEM((48, 128), BF16),
            pltpu.VMEM((3, 4, 4, 48, 128), BF16),
            pltpu.VMEM((4, NA, KD, 128), BF16),
            pltpu.VMEM((256, 256), F32),
            pltpu.VMEM((4, 256, 256), BF16),
            pltpu.VMEM((4, NA, 64, 128), BF16),
            pltpu.VMEM((4, NA, 64, 128), BF16),
            pltpu.VMEM((NA * 256, 128), F32),
            pltpu.VMEM((NK, NQ, 480), BF16),
            pltpu.VMEM((NK, NQ, 128), BF16),
            pltpu.VMEM((4, 16, 128), F32),
            pltpu.VMEM((4, 16, 128), F32),
            dma, dma, dma((12,)), dma((4, 4)), dma((3, 2)), dma((3, 2)),
            dma((4, CH)), dma((4, CH)), dma((3, CH)), dma((3, CH)), dma((3,)), dma((3,)),
        ],
        compiler_params=pltpu.CompilerParams(
            collective_id=0, has_side_effects=True, vmem_limit_bytes=48 << 20
        ),
    )(
        amp_old, lad, cycle_int, virt_irrep, virt_energy,
        virt_irrep.reshape(1, 480), occ_energy.reshape(1, 60), virt_energy.reshape(1, 480),
    )
    return amps.transpose(1, 0, 2)[None], cyc[None]


def solution(mesh):
    placed = (P("row", None, "dep"), P("row", "col", None, "dep"), P(), P(), P(), P())
    return jax.shard_map(
        on_device,
        mesh=mesh,
        in_specs=placed,
        out_specs=(P(("col", "dep"), None, "row", None), P(("col", "dep"), "row", None)),
        check_vma=False,
    )
```

time: 280 us -> 76.9 us (0.27)
  blocking collectives: 132 us -> 0 us
  waiting for transfers between devices: 90.8 us -> 0 us
  Pallas kernels: 0 us -> 68.2 us
  local copies, waits for them, and re-layouts: 28.3 us -> 7.33 us
  between operations: 14.1 us -> 0.65 us
  other arithmetic: 7.54 us -> 0 us
  matrix products: 5.09 us -> 0 us
    all_gather x1 -> x0, blocking collectives: 107 us -> none  [on_device(): piece = lax.all_gather(amp_old, 'row', axis=0, tiled=True)]
    unnamed x2 -> x0, waiting for transfers between devices: 90.8 us -> none
    pallas_call x0 -> x1, Pallas kernels: none -> 68.2 us  [on_device(): pl.pallas_call(kernel, name='ladder', out_shape=(jax.ShapeDtypeStruct((NA...]
    all_to_all x1 -> x0, blocking collectives: 24.4 us -> none  [on_device(): moved = lax.all_to_all(amps, 'col', split_axis=0, concat_axis=5, tiled=True)]
    convert_element_type x3 -> x0, local copies, waits for them, and re-layouts: 18.5 us -> none  [the longest x2 18.4 us: on_device(): partial_sums.astype(jnp.bfloat16)]
    dot_general x2 -> x0, matrix products: 5.09 us -> none  [the longest x1 3.22 us: on_device(): jnp.einsum('ikac,kqc->iaq', new_amps, cycle_int, preferred_element_type=j...]
    select_n x2 -> x0, other arithmetic: 5.04 us -> none  [the longest x1 5.03 us: on_device(): masked = jnp.where(sym, ladder_int, jnp.zeros((), jnp.bfloat16))]
    unnamed x8 -> x14, local copies, waits for them, and re-layouts: 2.55 us -> 7.33 us
  transfers between devices with their start and end apart: 1 -> 0, of which waited for: 1 -> 0; matrix products, arithmetic and copies ran while one was open for 1% -> 0% of each run, Pallas kernels for 0% -> 0%
where the time goes in v1:
time: 76.9 us; the launch traced here: 76.2 us
  Pallas kernels  68.2 us (89%)
  local copies, waits for them, and re-layouts  7.33 us (10%)
    pallas_call x1, Pallas kernels, on_device(): pl.pallas_call(kernel, name='ladder', out_shape=(jax.ShapeDtypeStruct((NA...  68.2 us
    unnamed x14, local copies, waits for them, and re-layouts  7.33 us

profile of v1, /device:TPU:1, one launch (start us, length us, event | category | flops | bytes accessed | tf_op | source)
XLA Modules:
  0.0 76.2 jit_solution(5646445548473356940)
XLA Ops:
  0.6 0.0 copy-start
  0.6 2.1 %copy-done = bf16[60,64,480]{2,1,0:T(8,128)(2,1)S(1)} copy-done((bf16[60,64,480]{2,1,0:T(8,128)(2,1)S(1)}, bf16[60,64,480]{2,1,0:T(8,128)(2,1)}, u32[]{:S(2)}) %copy-start) | copy-done | bytes 3686424
  2.7 0.0 copy-start.1
  2.7 1.1 %copy-done.1 = bf16[10,120,2,120]{3,2,1,0:T(2,128)(2,1)S(1)} copy-done((bf16[10,120,2,120]{3,2,1,0:T(2,128)(2,1)S(1)}, bf16[10,120,2,120]{3,2,1,0:T(2,128)(2,1)}, u32[]{:S(2)}) %copy-start.1) | copy-done | bytes 576024
  3.8 0.0 copy-start.2
  3.8 0.7 copy-done.2
  4.5 0.0 copy-start.3
  4.5 0.7 copy-done.3
  5.2 0.0 copy-start.4
  5.2 0.7 copy-done.4
  5.9 0.0 copy-start.5
  5.9 0.7 copy-done.5
  6.5 68.2 %ladder.1 = (bf16[10,60,480]{2,1,0:T(8,128)(2,1)S(1)}, f32[10,64]{1,0:T(8,128)S(1)}) custom-call(bf16[20,2,120]{2,1,0:T(2,128)(2,1)S(1)} %copy-done.2, bf16[2400,120]{1,0:T(8,128)(2,1)S(1)} %bitcast.9, bf16[60,64,480]{2,1,0:T(8,128)(2,1)S(1)} %copy-done, s32[480]{0:T(512)S(1)} %copy-done.3, f32[480]{0:T(512)S(1)} %copy-done.4, s32[1,480]{1,0:T(1,128)S(1)} %bitcast.10, ...), custom_call_target="tpu_custom_call" | custom-call | tf_op jit(solution)/shard_map/ladder/pallas_call | solution.py:385
  74.8 0.6 copy.8
  75.4 0.8 %copy.10 = bf16[1,60,10,480]{3,1,2,0:T(8,128)(2,1)} copy(bf16[1,60,10,480]{3,1,2,0:T(8,128)(2,1)S(1)} %bitcast.8) | data formatting | bytes 1152000
Async XLA Ops:
  0.6 2.1 %copy-start = (bf16[60,64,480]{2,1,0:T(8,128)(2,1)S(1)}, bf16[60,64,480]{2,1,0:T(8,128)(2,1)}, u32[]{:S(2)}) copy-start(bf16[60,64,480]{2,1,0:T(8,128)(2,1)} %cyc_hbm.1) | copy-start | bytes 11059204
  2.7 1.1 %copy-start.1 = (bf16[10,120,2,120]{3,2,1,0:T(2,128)(2,1)S(1)}, bf16[10,120,2,120]{3,2,1,0:T(2,128)(2,1)}, u32[]{:S(2)}) copy-start(bf16[10,120,2,120]{3,2,1,0:T(2,128)(2,1)} %param.7) | copy-start | bytes 1728004
  3.8 0.7 copy-start.2
  4.5 0.7 copy-start.3
  5.2 0.7 copy-start.4
  5.9 0.7 copy-start.5

commit v2 on v1

v2 whole, which is shorter than its diff:
```python
import jax
import jax.numpy as jnp
from jax import lax
from jax.experimental import pallas as pl
from jax.experimental.pallas import tpu as pltpu
from jax.sharding import PartitionSpec as P

MESH = pl.DeviceIdType.MESH
F32 = jnp.float32
BF16 = jnp.bfloat16
NX, NY, NZ = 4, 4, 12
NA, NB_, ND, NK, NQ = 10, 120, 120, 60, 64
CH = 5
KD = 2 * ND


def kernel(
    amp_hbm, lad_hbm, cyc_hbm, irr_hbm, occ_hbm, ene_hbm,
    out_ref, z_ref,
    amp_ref, lad_ref, irr_ref, occ_ref, ene_ref, vec_f, vec_i, shard, sh_all, lt, a_f, a_b, nb, rb, of, cyc, crot, zp, zr,
    in_sem, own_sem, s1_send, s1_recv, s2_send, s2_recv, b_send, b_recv, x_send, x_recv, e_send, e_recv, z_send, z_recv,
):
    row = lax.axis_index("row")
    col = lax.axis_index("col")
    x = lax.axis_index("dep")
    z = row // 4
    y = row % 4
    yh = col // 2
    core = col % 2

    def dev(zz, yy, cc, xx):
        return (zz * 4 + yy, cc, xx)

    r12 = 4 * (z % 3) + y
    xt = r12 // 3
    s_mine = r12 % 3
    ip_mine = z // 3
    s_here = (x + y) % 4
    z_off = (3 * x + s_here) // 4
    relay = s_here < 3

    left = (x + 3) % 4
    right = (x + 1) % 4
    diag = (x + 2) % 4

    barrier = pltpu.get_barrier_semaphore()

    def parity(s):
        return (core + (3 * x + s) // 4 + z) % 2

    def signal(d):
        pl.semaphore_signal(barrier, inc=1, device_id=d, device_id_type=MESH)

    @pl.when(relay)
    def _():
        def go(n, carry):
            zz = 3 * (2 * (n // 4) + parity(s_here)) + z_off
            xx = n % 4

            @pl.when(jnp.logical_or(zz != z, xx != x))
            def _():
                signal(dev(zz, y, col, xx))

            return carry

        lax.fori_loop(0, 8, go, 0)

    for t in range(1, 4):
        signal(dev(z, (y + t) % 4, col, x))
    signal(dev(z, y, col, left))
    signal(dev(z, y, col, right))
    for t in range(1, 4):
        signal(dev(z, y, (col + t) % 4, x))

    loads = [
        pltpu.make_async_copy(src, dst, in_sem.at[n])
        for n, (src, dst) in enumerate(
            [(amp_hbm, amp_ref), (irr_hbm, irr_ref), (occ_hbm, occ_ref), (ene_hbm, ene_ref), (lad_hbm, lad_ref), (cyc_hbm, cyc)]
        )
    ]
    for copy in loads:
        copy.start()
    cyc_copy = loads[5]
    a_f[...] = jnp.zeros_like(a_f)
    of[NA * 256:, :] = jnp.zeros((6 * 256, 128), F32)
    for copy in loads[:4]:
        copy.wait()

    raw = amp_ref[...]
    wide = jnp.concatenate(
        [raw[:, 0, :].astype(F32), raw[:, 1, :].astype(F32), jnp.zeros((20, 16), F32)], axis=1
    )
    gap = jnp.zeros((4, 128), F32)
    shard[...] = jnp.concatenate([wide[:, :128], gap, wide[:, 128:], gap], axis=0).astype(BF16)

    vec_f[...] = jnp.zeros_like(vec_f)
    vec_i[...] = jnp.zeros_like(vec_i)
    vec_f[0:1, 0:480] = ene_ref[...]
    vec_f[1:2, 0:60] = occ_ref[...]
    vec_i[0:1, 0:480] = irr_ref[...]
    lane = lax.broadcasted_iota(jnp.int32, (1, 128), 1)
    edge = 120 - 8 * col
    prev = jnp.maximum(col - 1, 0)
    at = pl.multiple_of(col * 128, 128)
    before = pl.multiple_of(prev * 128, 128)
    ene_b = jnp.where(lane < edge, vec_f[0:1, pl.ds(at, 128)], vec_f[0:1, pl.ds(before, 128)])
    irr_b = jnp.where(lane < edge, vec_i[0:1, pl.ds(at, 128)], vec_i[0:1, pl.ds(before, 128)])
    ii = lax.broadcasted_iota(jnp.int32, (ND, 512), 0)
    jj = lax.broadcasted_iota(jnp.int32, (ND, 512), 1)
    irr_d = jnp.sum(jnp.where(jj == ii + ND * x, vec_i[0:1, :].astype(F32), 0.0), axis=1, keepdims=True).astype(jnp.int32)
    pi = lax.broadcasted_iota(jnp.int32, (128, 128), 0)
    pj = lax.broadcasted_iota(jnp.int32, (128, 128), 1)
    occ_row = vec_f[1:2, 0:128]
    wide_lane = lax.broadcasted_iota(jnp.int32, (1, 512), 1)

    def ene_of(a):
        return jnp.sum(jnp.where(wide_lane == row * NA + a, vec_f[0:1, :], 0.0), axis=1, keepdims=True)

    def irr_of(n):
        picked = jnp.sum(jnp.where(wide_lane == n, vec_i[0:1, :].astype(F32), 0.0), axis=1, keepdims=True)
        return picked.astype(jnp.int32)

    irr_c = [irr_of(c) for c in range(2)]

    def occ_i_of(half):
        return jnp.sum(jnp.where(pj == (2 * half + pi // 64) * 4 + x, occ_row, 0.0), axis=1, keepdims=True)

    occ_k = jnp.sum(jnp.where(pj == pi % 64, occ_row, 0.0), axis=1, keepdims=True)
    occ_half = [occ_i_of(1 - yh) + occ_k, occ_i_of(yh) + occ_k]

    sr = lax.broadcasted_iota(jnp.int32, (2 * NB_, 256), 0)
    sc = lax.broadcasted_iota(jnp.int32, (2 * NB_, 256), 1)
    want_b = (sc % 128 + 8 * col) % 128
    pick = jnp.where(sr == 2 * want_b + sc // 128, 1.0, 0.0).astype(BF16)

    def prep(a, carry):
        block = lad_ref[pl.ds(pl.multiple_of(a * 240, 240), 240), :]
        got = lax.dot_general(block, pick, (((0,), (0,)), ((), ())), preferred_element_type=F32)
        ab = jnp.bitwise_xor(irr_b, irr_of(row * NA + a))
        both = []
        for c in range(2):
            keep = jnp.bitwise_xor(ab, irr_c[c]) == irr_d
            both.append(jnp.where(keep, got[:, c * 128:(c + 1) * 128], 0.0))
        lt[x, a] = jnp.concatenate(both, axis=0).astype(BF16)
        return carry

    loads[4].wait()
    lax.fori_loop(0, NA, prep, 0)

    pl.semaphore_wait(barrier, 8 + 6 - jnp.where(jnp.logical_and(xt == x, core == 0), 1, 0))

    def s1_plane(n):
        even = jnp.where(n == 0, 6, jnp.where(n == 1, 8, jnp.where(n == 2, 4, jnp.where(n == 3, 10, jnp.where(n == 4, 2, 0)))))
        odd = jnp.where(n == 0, 5, jnp.where(n == 1, 7, jnp.where(n == 2, 3, jnp.where(n == 3, 9, jnp.where(n == 4, 1, 11)))))
        return (z + jnp.where(core == 0, even, odd)) % 12

    def s1_copy(n):
        zz = s1_plane(n)
        return pltpu.make_async_remote_copy(
            src_ref=shard, dst_ref=sh_all.at[s_mine, ip_mine, x],
            send_sem=s1_send.at[n], recv_sem=s1_recv.at[ip_mine, x],
            device_id=dev(zz, y, col, xt), device_id_type=MESH,
        )

    def s1_here(n):
        return jnp.logical_and(s1_plane(n) == z, xt == x)

    stays = jnp.logical_and(xt == x, core == 0)

    def s1_go(n, carry):
        @pl.when(jnp.logical_not(s1_here(n)))
        def _():
            s1_copy(n).start()

        return carry

    lax.fori_loop(0, 6, s1_go, 0)

    @pl.when(stays)
    def _():
        pltpu.make_async_copy(shard, sh_all.at[s_mine, ip_mine, x], own_sem).start()

    def x_own(j, side):
        return pltpu.make_async_remote_copy(
            src_ref=lt.at[x, pl.ds(2 * j, 2)], dst_ref=lt.at[x, pl.ds(2 * j, 2)],
            send_sem=x_send.at[side, j], recv_sem=x_recv.at[side, j],
            device_id=dev(z, y, col, left if side == 0 else right), device_id_type=MESH,
        )

    def x_fwd(j, side):
        owner = right if side == 0 else left
        a = 2 * j + (1 if side == 0 else 0)
        return pltpu.make_async_remote_copy(
            src_ref=lt.at[owner, a], dst_ref=lt.at[owner, a],
            send_sem=x_send.at[2 + side, j], recv_sem=x_recv.at[2 + side, j],
            device_id=dev(z, y, col, left if side == 0 else right), device_id_type=MESH,
        )

    for j in range(3):
        x_own(j, 0).start()
        x_own(j, 1).start()

    cyc_copy.wait()
    lane3 = lax.broadcasted_iota(jnp.int32, (1, 1, 128), 2)
    for t in range(4):
        @pl.when(col == t)
        def _():
            def rot(m, carry):
                lo = max(t - 1, 0) * 128
                for u in range(2):
                    k = 2 * m + u
                    if t < 3:
                        here = cyc[pl.ds(k, 1), :, t * 128:(t + 1) * 128]
                    else:
                        here = jnp.concatenate(
                            [cyc[pl.ds(k, 1), :, 384:480], cyc[pl.ds(k, 1), :, 352:384]], axis=2
                        )
                    there = cyc[pl.ds(k, 1), :, lo:lo + 128]
                    crot[pl.ds(m, 1), :, u * 128:(u + 1) * 128] = jnp.where(lane3 < 120 - 8 * t, here, there)
                return carry

            lax.fori_loop(0, NK // 2, rot, 0)

    def unit(s, h, mine):
        half = (1 - yh) if h == 0 else yh
        share = parity(s) if mine else 1 - parity(s)
        return sh_all.at[s, 2 * half + share]

    def s2_copy(t, h):
        return pltpu.make_async_remote_copy(
            src_ref=unit(s_here, h, True), dst_ref=unit(s_here, h, True),
            send_sem=s2_send.at[t - 1, h], recv_sem=s2_recv.at[s_here, h],
            device_id=dev(z, (y + t) % 4, col, x), device_id_type=MESH,
        )

    def s2_wait(s, h):
        return pltpu.make_async_remote_copy(
            src_ref=unit(s, h, True), dst_ref=unit(s, h, True),
            send_sem=s2_send.at[0, h], recv_sem=s2_recv.at[s, h],
            device_id=dev(z, (y + 1) % 4, col, x), device_id_type=MESH,
        )

    other = 2 * yh + 1 - core

    def sib_copy(s, h):
        return pltpu.make_async_remote_copy(
            src_ref=unit(s, h, True), dst_ref=unit(s, h, True),
            send_sem=b_send.at[s, h], recv_sem=b_recv.at[s, h],
            device_id=dev(z, y, other, x), device_id_type=MESH,
        )

    def sib_wait(s, h):
        return pltpu.make_async_remote_copy(
            src_ref=unit(s, h, False), dst_ref=unit(s, h, False),
            send_sem=b_send.at[s, h], recv_sem=b_recv.at[s, h],
            device_id=dev(z, y, other, x), device_id_type=MESH,
        )

    def forward(j):
        x_own(j, 0).wait_recv()
        x_own(j, 1).wait_recv()
        x_fwd(j, 0).start()
        x_fwd(j, 1).start()
        if j + 3 < CH:
            x_own(j + 3, 0).start()
            x_own(j + 3, 1).start()

    forward(0)

    @pl.when(stays)
    def _():
        pltpu.make_async_copy(shard, sh_all.at[s_mine, ip_mine, x], own_sem).wait()

    @pl.when(relay)
    def _():
        for h in range(2):
            half = (1 - yh) if h == 0 else yh
            i4 = 2 * half + parity(s_here)
            zz = 3 * i4 + z_off

            def got(xx, carry):
                @pl.when(jnp.logical_or(zz != z, xx != x))
                def _():
                    pltpu.make_async_remote_copy(
                        src_ref=shard, dst_ref=sh_all.at[s_here, i4, xx],
                        send_sem=s1_send.at[0], recv_sem=s1_recv.at[i4, xx],
                        device_id=dev(z, y, other, x), device_id_type=MESH,
                    ).wait_recv()

                return carry

            lax.fori_loop(0, 4, got, 0)
            for t in (2, 1, 3):
                s2_copy(t, h).start()
            sib_copy(s_here, h).start()

    def pass_on(h):
        for s in range(3):
            @pl.when(s_here != s)
            def _():
                s2_wait(s, h).wait_recv()
                sib_copy(s, h).start()

    def operand(h):
        half = (1 - yh) if h == 0 else yh
        for s in range(3):
            sib_wait(s, h).wait_recv()
        base = pl.multiple_of(half * 128, 128)
        for xx in range(4):
            for n in range(2):
                for s in range(3):
                    got = sh_all[s, 2 * half + n, xx].astype(F32)
                    top = n * 64 + s * 20
                    a_f[top:top + 20, 0:128] = got[0:20]
                    a_f[top:top + 20, 128:256] = got[24:44]
            a_b[xx, pl.ds(base, 128), :] = a_f[...].astype(BF16)

    forward(1)
    pass_on(0)
    pass_on(1)
    forward(2)
    operand(0)

    partners = [(2, 0), (2, 1), (0, 1)]

    def e_copy(p, j):
        dh, dc = partners[p]
        to = ((yh * 2 + dh) % 4) + (core + dc) % 2
        return pltpu.make_async_remote_copy(
            src_ref=nb.at[to, pl.ds(2 * j, 2)], dst_ref=rb.at[col, pl.ds(2 * j, 2)],
            send_sem=e_send.at[p, j], recv_sem=e_recv.at[p, j],
            device_id=dev(z, y, to, x), device_id_type=MESH,
        )

    def e_wait(p, j):
        dh, dc = partners[p]
        frm = ((yh * 2 + dh) % 4) + (core + dc) % 2
        pltpu.make_async_remote_copy(
            src_ref=nb.at[frm, pl.ds(2 * j, 2)], dst_ref=rb.at[frm, pl.ds(2 * j, 2)],
            send_sem=e_send.at[p, j], recv_sem=e_recv.at[p, j],
            device_id=dev(z, y, frm, x), device_id_type=MESH,
        ).wait_recv()

    def block(j, h):
        half = (1 - yh) if h == 0 else yh
        base = pl.multiple_of(half * 128, 128)
        total = None
        for xx in range(4):
            w = jnp.concatenate([lt[xx, 2 * j], lt[xx, 2 * j + 1]], axis=1)
            term = jnp.dot(a_b[xx, pl.ds(base, 128), 0:KD], w, preferred_element_type=F32)
            total = term if total is None else total + term
        occ = occ_half[h]
        for g in range(2):
            a = 2 * j + g
            denom = (ene_of(a) + ene_b) - occ
            new = (total[:, g * 128:(g + 1) * 128] / denom).astype(BF16)
            nb[2 * half, a] = new[0:64]
            nb[2 * half + 1, a] = new[64:128]
            of[pl.ds(pl.multiple_of(a * 256 + half * 128, 128), 128), :] = new.astype(F32)
        for p in ((0, 1) if h == 0 else (2,)):
            e_copy(p, j).start()

    def diag_in(j):
        x_fwd(j, 0).wait_recv()
        x_fwd(j, 1).wait_recv()

    diag_in(0)
    block(0, 0)
    diag_in(1)
    block(1, 0)
    forward(3)
    operand(1)
    block(0, 1)
    block(1, 1)
    diag_in(2)
    block(2, 0)
    block(2, 1)
    forward(4)
    for j in range(3, CH):
        diag_in(j)
        block(j, 0)
        block(j, 1)

    rb[pl.ds(col, 1)] = nb[pl.ds(col, 1)]

    def cycle(m, acc):
        parts = []
        for u in range(2):
            rows = [of[pl.ds(i4 * 64 + 2 * m + u, 16, stride=256), :] for i4 in range(4)]
            parts.append(jnp.concatenate(rows, axis=0).astype(BF16))
        left_op = jnp.concatenate(parts, axis=1)
        return acc + lax.dot_general(left_op, crot[m], (((1,), (1,)), ((), ())), preferred_element_type=F32)

    zsum = lax.fori_loop(0, NK // 2, cycle, jnp.zeros((64, NQ), F32), unroll=5)
    zw = jnp.concatenate([zsum, jnp.zeros((64, 64), F32)], axis=1)
    for i4 in range(4):
        zp[i4] = zw[i4 * 16:(i4 + 1) * 16]
    zr[pl.ds(col, 1)] = zp[pl.ds(col, 1)]

    def z_copy(p):
        dh, dc = partners[p]
        to = ((yh * 2 + dh) % 4) + (core + dc) % 2
        return pltpu.make_async_remote_copy(
            src_ref=zp.at[to], dst_ref=zr.at[col],
            send_sem=z_send.at[p], recv_sem=z_recv.at[p],
            device_id=dev(z, y, to, x), device_id_type=MESH,
        )

    def z_wait(p):
        dh, dc = partners[p]
        frm = ((yh * 2 + dh) % 4) + (core + dc) % 2
        pltpu.make_async_remote_copy(
            src_ref=zp.at[frm], dst_ref=zr.at[frm],
            send_sem=z_send.at[p], recv_sem=z_recv.at[p],
            device_id=dev(z, y, frm, x), device_id_type=MESH,
        ).wait_recv()

    for p in range(3):
        z_copy(p).start()

    lane_o = lax.broadcasted_iota(jnp.int32, (1, 128), 1)
    for j in range(CH):
        for p in range(3):
            e_wait(p, j)
        for h in range(2):
            a = 2 * j + h
            for t in range(3):
                tile = jnp.where(lane_o < 120 - 8 * t, rb[t, a], rb[t + 1, a])
                out_ref[a, :, t * 128:(t + 1) * 128] = tile[:NK]
            out_ref[a, :, 384:480] = rb[3, a][:NK, :96]

    for p in range(3):
        z_wait(p)
    zt = (zr[0] + zr[1]) + (zr[2] + zr[3])
    z_ref[...] = zt[:NA, :NQ]

    def s1_done(n, carry):
        @pl.when(jnp.logical_not(s1_here(n)))
        def _():
            s1_copy(n).wait_send()

        return carry

    lax.fori_loop(0, 6, s1_done, 0)

    @pl.when(relay)
    def _():
        for h in range(2):
            for t in range(1, 4):
                s2_copy(t, h).wait_send()

    for h in range(2):
        for s in range(3):
            sib_copy(s, h).wait_send()

    for j in range(CH):
        for side in range(2):
            x_own(j, side).wait_send()
            x_fwd(j, side).wait_send()
        for p in range(3):
            e_copy(p, j).wait_send()
    for p in range(3):
        z_copy(p).wait_send()


def on_device(amp_old, ladder_int, cycle_int, virt_irrep, occ_energy, virt_energy):
    vmem = pl.BlockSpec(memory_space=pltpu.VMEM)
    hbm = pl.BlockSpec(memory_space=pltpu.HBM)
    dma = pltpu.SemaphoreType.DMA
    lad = ladder_int.reshape(2 * NA * NB_, ND)
    amps, cyc = pl.pallas_call(
        kernel,
        name="ladder",
        out_shape=(
            jax.ShapeDtypeStruct((NA, NK, 480), BF16),
            jax.ShapeDtypeStruct((NA, NQ), F32),
        ),
        in_specs=[hbm] * 6,
        out_specs=(vmem, vmem),
        scratch_shapes=[
            pltpu.VMEM((20, 2, ND), BF16),
            pltpu.VMEM((2 * NA * NB_, ND), BF16),
            pltpu.VMEM((1, 480), jnp.int32),
            pltpu.VMEM((1, NK), F32),
            pltpu.VMEM((1, 480), F32),
            pltpu.VMEM((8, 512), F32),
            pltpu.VMEM((8, 512), jnp.int32),
            pltpu.VMEM((48, 128), BF16),
            pltpu.VMEM((3, 4, 4, 48, 128), BF16),
            pltpu.VMEM((4, NA, KD, 128), BF16),
            pltpu.VMEM((128, 256), F32),
            pltpu.VMEM((4, 256, 256), BF16),
            pltpu.VMEM((4, NA, 64, 128), BF16),
            pltpu.VMEM((4, NA, 64, 128), BF16),
            pltpu.VMEM((16 * 256, 128), F32),
            pltpu.VMEM((NK, NQ, 480), BF16),
            pltpu.VMEM((NK // 2, NQ, 256), BF16),
            pltpu.VMEM((4, 16, 128), F32),
            pltpu.VMEM((4, 16, 128), F32),
            dma((6,)), dma, dma((6,)), dma((4, 4)), dma((3, 2)), dma((3, 2)), dma((3, 2)), dma((3, 2)),
            dma((4, CH)), dma((4, CH)), dma((3, CH)), dma((3, CH)), dma((3,)), dma((3,)),
        ],
        compiler_params=pltpu.CompilerParams(
            collective_id=0, has_side_effects=True, vmem_limit_bytes=60 << 20
        ),
    )(
        amp_old, lad, cycle_int,
        virt_irrep.reshape(1, 480), occ_energy.reshape(1, 60), virt_energy.reshape(1, 480),
    )
    return amps.transpose(1, 0, 2)[None], cyc[None]


def solution(mesh):
    placed = (P("row", None, "dep"), P("row", "col", None, "dep"), P(), P(), P(), P())
    return jax.shard_map(
        on_device,
        mesh=mesh,
        in_specs=placed,
        out_specs=(P(("col", "dep"), None, "row", None), P(("col", "dep"), "row", None)),
        check_vma=False,
    )
```

time: 76.9 us -> 59.5 us (0.77)
  Pallas kernels: 68.2 us -> 55.3 us
  local copies, waits for them, and re-layouts: 7.33 us -> 3.26 us
    pallas_call x1, Pallas kernels: 68.2 us -> 55.3 us  [on_device(): pl.pallas_call(kernel, name='ladder', out_shape=(jax.ShapeDtypeStruct((NA...]
    unnamed x14 -> x2, local copies, waits for them, and re-layouts: 7.33 us -> 3.26 us
where the time goes in v2:
time: 59.5 us; the launch traced here: 59.2 us
  Pallas kernels  55.3 us (93%)
  local copies, waits for them, and re-layouts  3.26 us (5%)
  between operations  0.64 us (1%)
    pallas_call x1, Pallas kernels, on_device(): pl.pallas_call(kernel, name='ladder', out_shape=(jax.ShapeDtypeStruct((NA...  55.3 us
    unnamed x2, local copies, waits for them, and re-layouts  3.26 us

profile of v2, /device:TPU:1, one launch (start us, length us, event | category | flops | bytes accessed | tf_op | source)
XLA Modules:
  0.0 59.2 jit_solution(5058604121634106490)
XLA Ops:
  0.6 55.3 %ladder.1 = (bf16[10,60,480]{2,1,0:T(8,128)(2,1)}, f32[10,64]{1,0:T(8,128)}) custom-call(bf16[20,2,120]{2,1,0:T(2,128)(2,1)} %amp_hbm.1, bf16[2400,120]{1,0:T(8,128)(2,1)} %bitcast.9, bf16[60,64,480]{2,1,0:T(8,128)(2,1)} %cyc_hbm.1, s32[1,480]{1,0:T(1,128)} %bitcast.11, f32[1,60]{1,0:T(1,128)} %bitcast.13, f32[1,480]{1,0:T(1,128)} %bitcast.12), custom_call_target="tpu_custom_call" | custom-call | tf_op jit(solution)/shard_map/ladder/pallas_call | solution.py:471
  56.0 1.3 %copy.8 = f32[1,10,64]{2,0,1:T(1,128)} copy(f32[1,10,64]{2,1,0:T(8,128)} %bitcast.10) | data formatting | bytes 5120
  57.3 2.0 %copy.10 = bf16[1,60,10,480]{3,1,2,0:T(8,128)(2,1)} copy(bf16[1,60,10,480]{3,1,2,0:T(8,128)(2,1)} %bitcast.8) | data formatting | bytes 1152000

commit v3 on v2

--- a/solution.py
+++ b/solution.py
@@ -16,9 +16,9 @@
 
 def kernel(
     amp_hbm, lad_hbm, cyc_hbm, irr_hbm, occ_hbm, ene_hbm,
-    out_ref, z_ref,
-    amp_ref, lad_ref, irr_ref, occ_ref, ene_ref, vec_f, vec_i, shard, sh_all, lt, a_f, a_b, nb, rb, of, cyc, crot, zp, zr,
-    in_sem, own_sem, s1_send, s1_recv, s2_send, s2_recv, b_send, b_recv, x_send, x_recv, e_send, e_recv, z_send, z_recv,
+    out_hbm, z_hbm,
+    out_ref, z_ref, amp_ref, lad_ref, irr_ref, occ_ref, ene_ref, vec_f, vec_i, shard, sh_all, lt, a_f, a_b, nb, rb, of, cyc, crot, zp, zr,
+    in_sem, out_sem, own_sem, s1_send, s1_recv, s2_send, s2_recv, b_send, b_recv, x_send, x_recv, e_send, e_recv, z_send, z_recv,
 ):
     row = lax.axis_index("row")
     col = lax.axis_index("col")
@@ -81,10 +81,7 @@
     for copy in loads:
         copy.start()
     cyc_copy = loads[5]
-    a_f[...] = jnp.zeros_like(a_f)
-    of[NA * 256:, :] = jnp.zeros((6 * 256, 128), F32)
-    for copy in loads[:4]:
-        copy.wait()
+    loads[0].wait()
 
     raw = amp_ref[...]
     wide = jnp.concatenate(
@@ -92,6 +89,9 @@
     )
     gap = jnp.zeros((4, 128), F32)
     shard[...] = jnp.concatenate([wide[:, :128], gap, wide[:, 128:], gap], axis=0).astype(BF16)
+
+    for copy in loads[1:4]:
+        copy.wait()
 
     vec_f[...] = jnp.zeros_like(vec_f)
     vec_i[...] = jnp.zeros_like(vec_i)
@@ -108,9 +108,6 @@
     ii = lax.broadcasted_iota(jnp.int32, (ND, 512), 0)
     jj = lax.broadcasted_iota(jnp.int32, (ND, 512), 1)
     irr_d = jnp.sum(jnp.where(jj == ii + ND * x, vec_i[0:1, :].astype(F32), 0.0), axis=1, keepdims=True).astype(jnp.int32)
-    pi = lax.broadcasted_iota(jnp.int32, (128, 128), 0)
-    pj = lax.broadcasted_iota(jnp.int32, (128, 128), 1)
-    occ_row = vec_f[1:2, 0:128]
     wide_lane = lax.broadcasted_iota(jnp.int32, (1, 512), 1)
 
     def ene_of(a):
@@ -121,12 +118,6 @@
         return picked.astype(jnp.int32)
 
     irr_c = [irr_of(c) for c in range(2)]
-
-    def occ_i_of(half):
-        return jnp.sum(jnp.where(pj == (2 * half + pi // 64) * 4 + x, occ_row, 0.0), axis=1, keepdims=True)
-
-    occ_k = jnp.sum(jnp.where(pj == pi % 64, occ_row, 0.0), axis=1, keepdims=True)
-    occ_half = [occ_i_of(1 - yh) + occ_k, occ_i_of(yh) + occ_k]
 
     sr = lax.broadcasted_iota(jnp.int32, (2 * NB_, 256), 0)
     sc = lax.broadcasted_iota(jnp.int32, (2 * NB_, 256), 1)
@@ -144,9 +135,6 @@
         lt[x, a] = jnp.concatenate(both, axis=0).astype(BF16)
         return carry
 
-    loads[4].wait()
-    lax.fori_loop(0, NA, prep, 0)
-
     pl.semaphore_wait(barrier, 8 + 6 - jnp.where(jnp.logical_and(xt == x, core == 0), 1, 0))
 
     def s1_plane(n):
@@ -196,9 +184,24 @@
             device_id=dev(z, y, col, left if side == 0 else right), device_id_type=MESH,
         )
 
-    for j in range(3):
-        x_own(j, 0).start()
-        x_own(j, 1).start()
+    loads[4].wait()
+    for j in range(CH):
+        lax.fori_loop(2 * j, 2 * j + 2, prep, 0)
+        if j < 3:
+            x_own(j, 0).start()
+            x_own(j, 1).start()
+
+    a_f[...] = jnp.zeros_like(a_f)
+    of[NA * 256:, :] = jnp.zeros((6 * 256, 128), F32)
+    pi = lax.broadcasted_iota(jnp.int32, (128, 128), 0)
+    pj = lax.broadcasted_iota(jnp.int32, (128, 128), 1)
+    occ_row = vec_f[1:2, 0:128]
+    def occ_i_of(half):
+        return jnp.sum(jnp.where(pj == (2 * half + pi // 64) * 4 + x, occ_row, 0.0), axis=1, keepdims=True)
+
+    occ_k = jnp.sum(jnp.where(pj == pi % 64, occ_row, 0.0), axis=1, keepdims=True)
+    occ_half = [occ_i_of(1 - yh) + occ_k, occ_i_of(yh) + occ_k]
+
 
     cyc_copy.wait()
     lane3 = lax.broadcasted_iota(jnp.int32, (1, 1, 128), 2)
@@ -317,8 +320,6 @@
 
     forward(1)
     pass_on(0)
-    pass_on(1)
-    forward(2)
     operand(0)
 
     partners = [(2, 0), (2, 1), (0, 1)]
@@ -366,6 +367,8 @@
 
     diag_in(0)
     block(0, 0)
+    forward(2)
+    pass_on(1)
     diag_in(1)
     block(1, 0)
     forward(3)
@@ -418,6 +421,12 @@
     for p in range(3):
         z_copy(p).start()
 
+    def out_copy(j):
+        part = pl.ds(2 * j, 2)
+        return pltpu.make_async_copy(out_ref.at[part], out_hbm.at[part], out_sem.at[j])
+
+    z_out = pltpu.make_async_copy(z_ref, z_hbm, out_sem.at[CH])
+
     lane_o = lax.broadcasted_iota(jnp.int32, (1, 128), 1)
     for j in range(CH):
         for p in range(3):
@@ -428,11 +437,13 @@
                 tile = jnp.where(lane_o < 120 - 8 * t, rb[t, a], rb[t + 1, a])
                 out_ref[a, :, t * 128:(t + 1) * 128] = tile[:NK]
             out_ref[a, :, 384:480] = rb[3, a][:NK, :96]
+        out_copy(j).start()
 
     for p in range(3):
         z_wait(p)
     zt = (zr[0] + zr[1]) + (zr[2] + zr[3])
-    z_ref[...] = zt[:NA, :NQ]
+    z_ref[:, 0, :] = zt[:NA, :NQ]
+    z_out.start()
 
     def s1_done(n, carry):
         @pl.when(jnp.logical_not(s1_here(n)))
@@ -461,23 +472,42 @@
             e_copy(p, j).wait_send()
     for p in range(3):
         z_copy(p).wait_send()
+    for j in range(CH):
+        out_copy(j).wait()
+    z_out.wait()
+
+
+def hand_on(amps_in, cyc_in, amps_out, cyc_out, amps, cyc, sem_in, sem_out):
+    refs = [(amps_in.at[pl.ds(2 * j, 2)], amps.at[pl.ds(2 * j, 2)], amps_out.at[pl.ds(2 * j, 2)]) for j in range(CH)]
+    refs.append((cyc_in, cyc, cyc_out))
+    reads = [pltpu.make_async_copy(src, mid, sem_in.at[n]) for n, (src, mid, _) in enumerate(refs)]
+    writes = [pltpu.make_async_copy(mid, dst, sem_out.at[n]) for n, (_, mid, dst) in enumerate(refs)]
+    for copy in reads:
+        copy.start()
+    for read, write in zip(reads, writes):
+        read.wait()
+        write.start()
+    for copy in writes:
+        copy.wait()
 
 
 def on_device(amp_old, ladder_int, cycle_int, virt_irrep, occ_energy, virt_energy):
-    vmem = pl.BlockSpec(memory_space=pltpu.VMEM)
     hbm = pl.BlockSpec(memory_space=pltpu.HBM)
     dma = pltpu.SemaphoreType.DMA
     lad = ladder_int.reshape(2 * NA * NB_, ND)
+    out_shape = (
+        jax.ShapeDtypeStruct((NA, NK, 480), BF16),
+        jax.ShapeDtypeStruct((NA, 1, NQ), F32),
+    )
     amps, cyc = pl.pallas_call(
         kernel,
         name="ladder",
-        out_shape=(
-            jax.ShapeDtypeStruct((NA, NK, 480), BF16),
-            jax.ShapeDtypeStruct((NA, NQ), F32),
-        ),
+        out_shape=out_shape,
         in_specs=[hbm] * 6,
-        out_specs=(vmem, vmem),
+        out_specs=(hbm, hbm),
         scratch_shapes=[
+            pltpu.VMEM((NA, NK, 480), BF16),
+            pltpu.VMEM((NA, 1, NQ), F32),
             pltpu.VMEM((20, 2, ND), BF16),
             pltpu.VMEM((2 * NA * NB_, ND), BF16),
             pltpu.VMEM((1, 480), jnp.int32),
@@ -497,7 +527,7 @@
             pltpu.VMEM((NK // 2, NQ, 256), BF16),
             pltpu.VMEM((4, 16, 128), F32),
             pltpu.VMEM((4, 16, 128), F32),
-            dma((6,)), dma, dma((6,)), dma((4, 4)), dma((3, 2)), dma((3, 2)), dma((3, 2)), dma((3, 2)),
+            dma((6,)), dma((6,)), dma, dma((6,)), dma((4, 4)), dma((3, 2)), dma((3, 2)), dma((3, 2)), dma((3, 2)),
             dma((4, CH)), dma((4, CH)), dma((3, CH)), dma((3, CH)), dma((3,)), dma((3,)),
         ],
         compiler_params=pltpu.CompilerParams(
@@ -507,7 +537,20 @@
         amp_old, lad, cycle_int,
         virt_irrep.reshape(1, 480), occ_energy.reshape(1, 60), virt_energy.reshape(1, 480),
     )
-    return amps.transpose(1, 0, 2)[None], cyc[None]
+    amps, cyc = pl.pallas_call(
+        hand_on,
+        name="hand_on",
+        out_shape=out_shape,
+        in_specs=[hbm, hbm],
+        out_specs=(hbm, hbm),
+        scratch_shapes=[
+            pltpu.VMEM((NA, NK, 480), BF16),
+            pltpu.VMEM((NA, 1, NQ), F32),
+            dma((CH + 1,)), dma((CH + 1,)),
+        ],
+        compiler_params=pltpu.CompilerParams(vmem_limit_bytes=60 << 20),
+    )(amps, cyc)
+    return amps.transpose(1, 0, 2)[None], cyc.transpose(1, 0, 2)
 
 
 def solution(mesh):

time: 59.5 us -> 57 us (0.958)
  local copies, waits for them, and re-layouts: 3.26 us -> 0 us
  Pallas kernels: 55.3 us -> 56.2 us
    unnamed x2 -> x0, local copies, waits for them, and re-layouts: 3.26 us -> none
    pallas_call x1 -> x2, Pallas kernels: 55.3 us -> 56.2 us  [the longest x1 54.2 us: on_device(): pl.pallas_call(kernel, name='ladder', out_shape=out_shape, in_specs=[hbm]...]
where the time goes in v3:
time: 57 us; the launch traced here: 56.8 us
  Pallas kernels  56.2 us (99%)
  between operations  0.64 us (1%)
    pallas_call x1, Pallas kernels, on_device(): pl.pallas_call(kernel, name='ladder', out_shape=out_shape, in_specs=[hbm]...  54.2 us
    pallas_call x1, Pallas kernels, on_device(): pl.pallas_call(hand_on, name='hand_on', out_shape=out_shape, in_specs=[hb...  1.93 us

profile of v3, /device:TPU:1, one launch (start us, length us, event | category | flops | bytes accessed | tf_op | source)
XLA Modules:
  0.0 56.8 jit_solution(8013923499834594781)
XLA Ops:
  0.6 54.2 %ladder.1 = (bf16[10,60,480]{2,1,0:T(8,128)(2,1)}, f32[10,1,64]{2,1,0:T(1,128)}) custom-call(bf16[20,2,120]{2,1,0:T(2,128)(2,1)} %amp_hbm.1, bf16[2400,120]{1,0:T(8,128)(2,1)} %bitcast.8, bf16[60,64,480]{2,1,0:T(8,128)(2,1)} %cyc_hbm.1, s32[1,480]{1,0:T(1,128)} %bitcast.9, f32[1,60]{1,0:T(1,128)} %bitcast.11, f32[1,480]{1,0:T(1,128)} %bitcast.10), custom_call_target="tpu_custom_call" | custom-call | tf_op jit(solution)/shard_map/ladder/pallas_call | solution.py:502
  54.9 1.9 %hand_on.1 = (bf16[10,60,480]{2,1,0:T(8,128)(2,1)}, f32[10,1,64]{2,1,0:T(1,128)}) custom-call(bf16[10,60,480]{2,1,0:T(8,128)(2,1)} %get-tuple-element.6.amps_in, f32[10,1,64]{2,1,0:T(1,128)} %get-tuple-element.7.cyc_in), custom_call_target="tpu_custom_call" | custom-call | tf_op jit(solution)/shard_map/hand_on/pallas_call | solution.py:540

commit v4 on v3

--- a/solution.py
+++ b/solution.py
@@ -43,6 +43,15 @@
     right = (x + 1) % 4
     diag = (x + 2) % 4
 
+    loads = [
+        pltpu.make_async_copy(src, dst, in_sem.at[n])
+        for n, (src, dst) in enumerate(
+            [(amp_hbm, amp_ref), (irr_hbm, irr_ref), (occ_hbm, occ_ref), (ene_hbm, ene_ref), (lad_hbm, lad_ref), (cyc_hbm, cyc)]
+        )
+    ]
+    for copy in loads:
+        copy.start()
+    cyc_copy = loads[5]
     barrier = pltpu.get_barrier_semaphore()
 
     def parity(s):
@@ -72,15 +81,6 @@
     for t in range(1, 4):
         signal(dev(z, y, (col + t) % 4, x))
 
-    loads = [
-        pltpu.make_async_copy(src, dst, in_sem.at[n])
-        for n, (src, dst) in enumerate(
-            [(amp_hbm, amp_ref), (irr_hbm, irr_ref), (occ_hbm, occ_ref), (ene_hbm, ene_ref), (lad_hbm, lad_ref), (cyc_hbm, cyc)]
-        )
-    ]
-    for copy in loads:
-        copy.start()
-    cyc_copy = loads[5]
     loads[0].wait()
 
     raw = amp_ref[...]
@@ -89,6 +89,39 @@
     )
     gap = jnp.zeros((4, 128), F32)
     shard[...] = jnp.concatenate([wide[:, :128], gap, wide[:, 128:], gap], axis=0).astype(BF16)
+
+    pl.semaphore_wait(barrier, 8 + 6 - jnp.where(jnp.logical_and(xt == x, core == 0), 1, 0))
+
+    def s1_plane(n):
+        even = jnp.where(n == 0, 6, jnp.where(n == 1, 8, jnp.where(n == 2, 4, jnp.where(n == 3, 10, jnp.where(n == 4, 2, 0)))))
+        odd = jnp.where(n == 0, 5, jnp.where(n == 1, 7, jnp.where(n == 2, 3, jnp.where(n == 3, 9, jnp.where(n == 4, 1, 11)))))
+        return (z + jnp.where(core == 0, even, odd)) % 12
+
+    def s1_copy(n):
+        zz = s1_plane(n)
+        return pltpu.make_async_remote_copy(
+            src_ref=shard, dst_ref=sh_all.at[s_mine, ip_mine, x],
+            send_sem=s1_send.at[n], recv_sem=s1_recv.at[ip_mine, x],
+            device_id=dev(zz, y, col, xt), device_id_type=MESH,
+        )
+
+    def s1_here(n):
+        return jnp.logical_and(s1_plane(n) == z, xt == x)
+
+    stays = jnp.logical_and(xt == x, core == 0)
+
+    def s1_go(n, carry):
+        @pl.when(jnp.logical_not(s1_here(n)))
+        def _():
+            s1_copy(n).start()
+
+        return carry
+
+    lax.fori_loop(0, 6, s1_go, 0)
+
+    @pl.when(stays)
+    def _():
+        pltpu.make_async_copy(shard, sh_all.at[s_mine, ip_mine, x], own_sem).start()
 
     for copy in loads[1:4]:
         copy.wait()
@@ -134,39 +167,6 @@
             both.append(jnp.where(keep, got[:, c * 128:(c + 1) * 128], 0.0))
         lt[x, a] = jnp.concatenate(both, axis=0).astype(BF16)
         return carry
-
-    pl.semaphore_wait(barrier, 8 + 6 - jnp.where(jnp.logical_and(xt == x, core == 0), 1, 0))
-
-    def s1_plane(n):
-        even = jnp.where(n == 0, 6, jnp.where(n == 1, 8, jnp.where(n == 2, 4, jnp.where(n == 3, 10, jnp.where(n == 4, 2, 0)))))
-        odd = jnp.where(n == 0, 5, jnp.where(n == 1, 7, jnp.where(n == 2, 3, jnp.where(n == 3, 9, jnp.where(n == 4, 1, 11)))))
-        return (z + jnp.where(core == 0, even, odd)) % 12
-
-    def s1_copy(n):
-        zz = s1_plane(n)
-        return pltpu.make_async_remote_copy(
-            src_ref=shard, dst_ref=sh_all.at[s_mine, ip_mine, x],
-            send_sem=s1_send.at[n], recv_sem=s1_recv.at[ip_mine, x],
-            device_id=dev(zz, y, col, xt), device_id_type=MESH,
-        )
-
-    def s1_here(n):
-        return jnp.logical_and(s1_plane(n) == z, xt == x)
-
-    stays = jnp.logical_and(xt == x, core == 0)
-
-    def s1_go(n, carry):
-        @pl.when(jnp.logical_not(s1_here(n)))
-        def _():
-            s1_copy(n).start()
-
-        return carry
-
-    lax.fori_loop(0, 6, s1_go, 0)
-
-    @pl.when(stays)
-    def _():
-        pltpu.make_async_copy(shard, sh_all.at[s_mine, ip_mine, x], own_sem).start()
 
     def x_own(j, side):
         return pltpu.make_async_remote_copy(
@@ -319,6 +319,7 @@
             a_b[xx, pl.ds(base, 128), :] = a_f[...].astype(BF16)
 
     forward(1)
+    forward(2)
     pass_on(0)
     operand(0)
 
@@ -365,41 +366,6 @@
         x_fwd(j, 0).wait_recv()
         x_fwd(j, 1).wait_recv()
 
-    diag_in(0)
-    block(0, 0)
-    forward(2)
-    pass_on(1)
-    diag_in(1)
-    block(1, 0)
-    forward(3)
-    operand(1)
-    block(0, 1)
-    block(1, 1)
-    diag_in(2)
-    block(2, 0)
-    block(2, 1)
-    forward(4)
-    for j in range(3, CH):
-        diag_in(j)
-        block(j, 0)
-        block(j, 1)
-
-    rb[pl.ds(col, 1)] = nb[pl.ds(col, 1)]
-
-    def cycle(m, acc):
-        parts = []
-        for u in range(2):
-            rows = [of[pl.ds(i4 * 64 + 2 * m + u, 16, stride=256), :] for i4 in range(4)]
-            parts.append(jnp.concatenate(rows, axis=0).astype(BF16))
-        left_op = jnp.concatenate(parts, axis=1)
-        return acc + lax.dot_general(left_op, crot[m], (((1,), (1,)), ((), ())), preferred_element_type=F32)
-
-    zsum = lax.fori_loop(0, NK // 2, cycle, jnp.zeros((64, NQ), F32), unroll=5)
-    zw = jnp.concatenate([zsum, jnp.zeros((64, 64), F32)], axis=1)
-    for i4 in range(4):
-        zp[i4] = zw[i4 * 16:(i4 + 1) * 16]
-    zr[pl.ds(col, 1)] = zp[pl.ds(col, 1)]
-
     def z_copy(p):
         dh, dc = partners[p]
         to = ((yh * 2 + dh) % 4) + (core + dc) % 2
@@ -418,8 +384,47 @@
             device_id=dev(z, y, frm, x), device_id_type=MESH,
         ).wait_recv()
 
-    for p in range(3):
-        z_copy(p).start()
+    def cycle(h):
+        half = (1 - yh) if h == 0 else yh
+
+        def step(m, acc):
+            parts = []
+            for u in range(2):
+                rows = [of[pl.ds((2 * half + n) * 64 + 2 * m + u, 16, stride=256), :] for n in range(2)]
+                parts.append(jnp.concatenate(rows, axis=0).astype(BF16))
+            left_op = jnp.concatenate(parts, axis=1)
+            return acc + lax.dot_general(left_op, crot[m], (((1,), (1,)), ((), ())), preferred_element_type=F32)
+
+        zsum = lax.fori_loop(0, NK // 2, step, jnp.zeros((32, NQ), F32), unroll=6)
+        zw = jnp.concatenate([zsum, jnp.zeros((32, 64), F32)], axis=1)
+        for n in range(2):
+            zp[2 * half + n] = zw[n * 16:(n + 1) * 16]
+        for p in ((0, 1) if h == 0 else (2,)):
+            z_copy(p).start()
+
+    diag_in(0)
+    block(0, 0)
+    forward(3)
+    pass_on(1)
+    diag_in(1)
+    block(1, 0)
+    forward(4)
+    diag_in(2)
+    block(2, 0)
+    operand(1)
+    block(0, 1)
+    diag_in(3)
+    block(3, 0)
+    block(1, 1)
+    block(2, 1)
+    diag_in(4)
+    block(4, 0)
+    cycle(0)
+    block(3, 1)
+    block(4, 1)
+    cycle(1)
+    rb[pl.ds(col, 1)] = nb[pl.ds(col, 1)]
+    zr[pl.ds(col, 1)] = zp[pl.ds(col, 1)]
 
     def out_copy(j):
         part = pl.ds(2 * j, 2)

time: 57 us -> 56.7 us (level)
  no operation moved by 1% of the time
where the time goes in v4:
time: 56.7 us; the launch traced here: 56.6 us
  Pallas kernels  55.9 us (99%)
  between operations  0.64 us (1%)
    pallas_call x1, Pallas kernels, on_device(): pl.pallas_call(kernel, name='ladder', out_shape=out_shape, in_specs=[hbm]...  54 us
    pallas_call x1, Pallas kernels, on_device(): pl.pallas_call(hand_on, name='hand_on', out_shape=out_shape, in_specs=[hb...  1.93 us

profile of v4, /device:TPU:1, one launch (start us, length us, event | category | flops | bytes accessed | tf_op | source)
XLA Modules:
  0.0 56.6 jit_solution(16748413328428044661)
XLA Ops:
  0.6 54.0 %ladder.1 = (bf16[10,60,480]{2,1,0:T(8,128)(2,1)}, f32[10,1,64]{2,1,0:T(1,128)}) custom-call(bf16[20,2,120]{2,1,0:T(2,128)(2,1)} %amp_hbm.1, bf16[2400,120]{1,0:T(8,128)(2,1)} %bitcast.8, bf16[60,64,480]{2,1,0:T(8,128)(2,1)} %cyc_hbm.1, s32[1,480]{1,0:T(1,128)} %bitcast.9, f32[1,60]{1,0:T(1,128)} %bitcast.11, f32[1,480]{1,0:T(1,128)} %bitcast.10), custom_call_target="tpu_custom_call" | custom-call | tf_op jit(solution)/shard_map/ladder/pallas_call | solution.py:507
  54.6 1.9 %hand_on.1 = (bf16[10,60,480]{2,1,0:T(8,128)(2,1)}, f32[10,1,64]{2,1,0:T(1,128)}) custom-call(bf16[10,60,480]{2,1,0:T(8,128)(2,1)} %get-tuple-element.6.amps_in, f32[10,1,64]{2,1,0:T(1,128)} %get-tuple-element.7.cyc_in), custom_call_target="tpu_custom_call" | custom-call | tf_op jit(solution)/shard_map/hand_on/pallas_call | solution.py:545

commit v5 on v4

--- a/solution.py
+++ b/solution.py
@@ -17,7 +17,7 @@
 def kernel(
     amp_hbm, lad_hbm, cyc_hbm, irr_hbm, occ_hbm, ene_hbm,
     out_hbm, z_hbm,
-    out_ref, z_ref, amp_ref, lad_ref, irr_ref, occ_ref, ene_ref, vec_f, vec_i, shard, sh_all, lt, a_f, a_b, nb, rb, of, cyc, crot, zp, zr,
+    out_ref, z_ref, pick_ref, amp_ref, lad_ref, irr_ref, occ_ref, ene_ref, vec_f, vec_i, shard, sh_all, lt, a_f, a_b, nb, rb, of, cyc, crot, zp, zr,
     in_sem, out_sem, own_sem, s1_send, s1_recv, s2_send, s2_recv, b_send, b_recv, x_send, x_recv, e_send, e_recv, z_send, z_recv,
 ):
     row = lax.axis_index("row")
@@ -43,13 +43,19 @@
     right = (x + 1) % 4
     diag = (x + 2) % 4
 
+    def pick_matrix():
+        sr = lax.broadcasted_iota(jnp.int32, (2 * NB_, 256), 0)
+        sc = lax.broadcasted_iota(jnp.int32, (2 * NB_, 256), 1)
+        want_b = (sc % 128 + 8 * col) % 128
+        return jnp.where(sr == 2 * want_b + sc // 128, 1.0, 0.0).astype(BF16)
+
     loads = [
         pltpu.make_async_copy(src, dst, in_sem.at[n])
         for n, (src, dst) in enumerate(
-            [(amp_hbm, amp_ref), (irr_hbm, irr_ref), (occ_hbm, occ_ref), (ene_hbm, ene_ref), (lad_hbm, lad_ref), (cyc_hbm, cyc)]
+            [(amp_hbm, amp_ref), (lad_hbm, lad_ref), (irr_hbm, irr_ref), (occ_hbm, occ_ref), (ene_hbm, ene_ref), (cyc_hbm, cyc)]
         )
     ]
-    for copy in loads:
+    for copy in loads[:5]:
         copy.start()
     cyc_copy = loads[5]
     barrier = pltpu.get_barrier_semaphore()
@@ -81,6 +87,7 @@
     for t in range(1, 4):
         signal(dev(z, y, (col + t) % 4, x))
 
+    pick_ref[...] = pick_matrix()
     loads[0].wait()
 
     raw = amp_ref[...]
@@ -93,8 +100,8 @@
     pl.semaphore_wait(barrier, 8 + 6 - jnp.where(jnp.logical_and(xt == x, core == 0), 1, 0))
 
     def s1_plane(n):
-        even = jnp.where(n == 0, 6, jnp.where(n == 1, 8, jnp.where(n == 2, 4, jnp.where(n == 3, 10, jnp.where(n == 4, 2, 0)))))
-        odd = jnp.where(n == 0, 5, jnp.where(n == 1, 7, jnp.where(n == 2, 3, jnp.where(n == 3, 9, jnp.where(n == 4, 1, 11)))))
+        even = (6, 8, 4, 10, 2, 0)[n]
+        odd = (5, 7, 3, 9, 1, 11)[n]
         return (z + jnp.where(core == 0, even, odd)) % 12
 
     def s1_copy(n):
@@ -117,13 +124,14 @@
 
         return carry
 
-    lax.fori_loop(0, 6, s1_go, 0)
+    for n in range(6):
+        s1_go(n, 0)
 
     @pl.when(stays)
     def _():
         pltpu.make_async_copy(shard, sh_all.at[s_mine, ip_mine, x], own_sem).start()
 
-    for copy in loads[1:4]:
+    for copy in loads[2:5]:
         copy.wait()
 
     vec_f[...] = jnp.zeros_like(vec_f)
@@ -152,14 +160,9 @@
 
     irr_c = [irr_of(c) for c in range(2)]
 
-    sr = lax.broadcasted_iota(jnp.int32, (2 * NB_, 256), 0)
-    sc = lax.broadcasted_iota(jnp.int32, (2 * NB_, 256), 1)
-    want_b = (sc % 128 + 8 * col) % 128
-    pick = jnp.where(sr == 2 * want_b + sc // 128, 1.0, 0.0).astype(BF16)
-
     def prep(a, carry):
         block = lad_ref[pl.ds(pl.multiple_of(a * 240, 240), 240), :]
-        got = lax.dot_general(block, pick, (((0,), (0,)), ((), ())), preferred_element_type=F32)
+        got = lax.dot_general(block, pick_ref[...], (((0,), (0,)), ((), ())), preferred_element_type=F32)
         ab = jnp.bitwise_xor(irr_b, irr_of(row * NA + a))
         both = []
         for c in range(2):
@@ -184,7 +187,8 @@
             device_id=dev(z, y, col, left if side == 0 else right), device_id_type=MESH,
         )
 
-    loads[4].wait()
+    cyc_copy.start()
+    loads[1].wait()
     for j in range(CH):
         lax.fori_loop(2 * j, 2 * j + 2, prep, 0)
         if j < 3:
@@ -450,14 +454,10 @@
     z_ref[:, 0, :] = zt[:NA, :NQ]
     z_out.start()
 
-    def s1_done(n, carry):
+    for n in range(6):
         @pl.when(jnp.logical_not(s1_here(n)))
         def _():
             s1_copy(n).wait_send()
-
-        return carry
-
-    lax.fori_loop(0, 6, s1_done, 0)
 
     @pl.when(relay)
     def _():
@@ -513,6 +513,7 @@
         scratch_shapes=[
             pltpu.VMEM((NA, NK, 480), BF16),
             pltpu.VMEM((NA, 1, NQ), F32),
+            pltpu.VMEM((2 * NB_, 256), BF16),
             pltpu.VMEM((20, 2, ND), BF16),
             pltpu.VMEM((2 * NA * NB_, ND), BF16),
             pltpu.VMEM((1, 480), jnp.int32),

time: 56.7 us -> 56.9 us (level)
  no operation moved by 1% of the time
where the time goes in v5:
time: 56.9 us; the launch traced here: 56.7 us
  Pallas kernels  56.1 us (99%)
  between operations  0.64 us (1%)
    pallas_call x1, Pallas kernels, on_device(): pl.pallas_call(kernel, name='ladder', out_shape=out_shape, in_specs=[hbm]...  54.1 us
    pallas_call x1, Pallas kernels, on_device(): pl.pallas_call(hand_on, name='hand_on', out_shape=out_shape, in_specs=[hb...  1.93 us

profile of v5, /device:TPU:1, one launch (start us, length us, event | category | flops | bytes accessed | tf_op | source)
XLA Modules:
  0.0 56.7 jit_solution(12658859077874696951)
XLA Ops:
  0.6 54.1 %ladder.1 = (bf16[10,60,480]{2,1,0:T(8,128)(2,1)}, f32[10,1,64]{2,1,0:T(1,128)}) custom-call(bf16[20,2,120]{2,1,0:T(2,128)(2,1)} %amp_hbm.1, bf16[2400,120]{1,0:T(8,128)(2,1)} %bitcast.8, bf16[60,64,480]{2,1,0:T(8,128)(2,1)} %cyc_hbm.1, s32[1,480]{1,0:T(1,128)} %bitcast.9, f32[1,60]{1,0:T(1,128)} %bitcast.11, f32[1,480]{1,0:T(1,128)} %bitcast.10), custom_call_target="tpu_custom_call" | custom-call | tf_op jit(solution)/shard_map/ladder/pallas_call | solution.py:507
  54.8 1.9 %hand_on.1 = (bf16[10,60,480]{2,1,0:T(8,128)(2,1)}, f32[10,1,64]{2,1,0:T(1,128)}) custom-call(bf16[10,60,480]{2,1,0:T(8,128)(2,1)} %get-tuple-element.6.amps_in, f32[10,1,64]{2,1,0:T(1,128)} %get-tuple-element.7.cyc_in), custom_call_target="tpu_custom_call" | custom-call | tf_op jit(solution)/shard_map/hand_on/pallas_call | solution.py:546

commit v6 on v5

--- a/solution.py
+++ b/solution.py
@@ -415,10 +415,10 @@
     forward(4)
     diag_in(2)
     block(2, 0)
+    diag_in(3)
+    block(3, 0)
     operand(1)
     block(0, 1)
-    diag_in(3)
-    block(3, 0)
     block(1, 1)
     block(2, 1)
     diag_in(4)

time: 56.9 us -> 56.9 us (level)
  no operation moved by 1% of the time
where the time goes in v6:
time: 56.9 us; the launch traced here: 56.7 us
  Pallas kernels  56.1 us (99%)
  between operations  0.64 us (1%)
    pallas_call x1, Pallas kernels, on_device(): pl.pallas_call(kernel, name='ladder', out_shape=out_shape, in_specs=[hbm]...  54.1 us
    pallas_call x1, Pallas kernels, on_device(): pl.pallas_call(hand_on, name='hand_on', out_shape=out_shape, in_specs=[hb...  1.93 us

profile of v6, /device:TPU:1, one launch (start us, length us, event | category | flops | bytes accessed | tf_op | source)
XLA Modules:
  0.0 56.7 jit_solution(9052332548592896931)
XLA Ops:
  0.6 54.1 %ladder.1 = (bf16[10,60,480]{2,1,0:T(8,128)(2,1)}, f32[10,1,64]{2,1,0:T(1,128)}) custom-call(bf16[20,2,120]{2,1,0:T(2,128)(2,1)} %amp_hbm.1, bf16[2400,120]{1,0:T(8,128)(2,1)} %bitcast.8, bf16[60,64,480]{2,1,0:T(8,128)(2,1)} %cyc_hbm.1, s32[1,480]{1,0:T(1,128)} %bitcast.9, f32[1,60]{1,0:T(1,128)} %bitcast.11, f32[1,480]{1,0:T(1,128)} %bitcast.10), custom_call_target="tpu_custom_call" | custom-call | tf_op jit(solution)/shard_map/ladder/pallas_call | solution.py:507
  54.8 1.9 %hand_on.1 = (bf16[10,60,480]{2,1,0:T(8,128)(2,1)}, f32[10,1,64]{2,1,0:T(1,128)}) custom-call(bf16[10,60,480]{2,1,0:T(8,128)(2,1)} %get-tuple-element.6.amps_in, f32[10,1,64]{2,1,0:T(1,128)} %get-tuple-element.7.cyc_in), custom_call_target="tpu_custom_call" | custom-call | tf_op jit(solution)/shard_map/hand_on/pallas_call | solution.py:546
